TPU v7x, 32 devices: a whole 2x2x4 slice. The times are simulated.
32 devices in a mesh: lat: 4 (over z), lon: 8 (over y, x, core).
Axes of the slice: x: 2, y: 2, z: 4, core: 2. Of those that a mesh axis runs over, the one named last changes fastest.
Arguments:
- control: float32 [64, 64, 1024], P(None, 'lat', 'lon'), may hold values from -6 to 6
- kappa: float32 [2, 64, 1024], P(None, 'lat', 'lon'), may hold values from 0.08 to 0.24
- vert_sqrt: float32 [64, 64], replicated, may hold values from -0.75 to 0.75
- obs_tile: int32 [65536, 1], P(('lat', 'lon')), may hold values from 0 to 31; in each aligned block of 2048 rows (0 to 2047, 2048 to 4095, ...) at most 128 rows name the same one
- obs_cell: int32 [65536], P(('lat', 'lon')), may hold values from 0 to 2047
- obs_frac: float32 [2, 65536], P(None, ('lat', 'lon')), may hold values from 0 to 1
- obs_value: float32 [64, 65536], P(None, ('lat', 'lon')), may hold values from -6 to 6
- obs_precision: float32 [64, 65536], P(None, ('lat', 'lon')), may hold values from 0.25 to 4
Outputs:
- gradient: float32 [64, 64, 1024], P(None, 'lat', 'lon')
Inputs may be any that keep to these rules, and one draw needn't show every extreme that they name: `obs_tile`: among the profiles of one device, no tile is named by more than 128; some tile is named by exactly 128.
All inputs are finite; a program needn't handle non-finite values.
Results may differ from a plain program's by a relative error of at most 0.000067.
Values sent between devices are 32-bit elements; how exact they have to be, the bound alone decides.
A program may use at most 128 MiB of HBM per device.

v0:
```python
import jax
import jax.numpy as jnp
from jax import lax
from jax.sharding import PartitionSpec as P

STEPS = 4


def padded_2(cells, sides, width):
    for axis, dim in sides:
        count = lax.axis_size(axis)
        head = lax.slice_in_dim(cells, 0, width, axis=dim)
        tail = lax.slice_in_dim(cells, cells.shape[dim] - width, cells.shape[dim], axis=dim)
        cells = jnp.concatenate(
            [
                lax.ppermute(tail, axis, [(i, (i + 1) % count) for i in range(count)]),
                cells,
                lax.ppermute(head, axis, [((i + 1) % count, i) for i in range(count)]),
            ],
            axis=dim,
        )
    return cells


def from_behind(value, axis, steps):
    count = lax.axis_size(axis)
    pairs = [(source, (source + steps) % count) for source in range(count)]
    return lax.ppermute(value, axis, pairs)


def from_behind_2(value, axis, steps):
    count = lax.axis_size(axis)
    initial, last = (max(0, -steps), min(count, count - steps))
    return lax.ppermute(value, axis, [(source, source + steps) for source in range(initial, last)])


def diffuse_step(padded, coef_pad):
    center = padded[:, 1:-1, 1:-1]
    lon_coef = coef_pad[0]
    lat_coef = coef_pad[1]
    return (
        center
        + lon_coef[1:-1, 1:-1] * (padded[:, 1:-1, 2:] - center)
        + lon_coef[1:-1, :-2] * (padded[:, 1:-1, :-2] - center)
        + lat_coef[1:-1, 1:-1] * (padded[:, 2:, 1:-1] - center)
        + lat_coef[:-2, 1:-1] * (padded[:, :-2, 1:-1] - center)
    )


def per_device(control, kappa, vert_sqrt, obs_tile, obs_cell, obs_frac, obs_value, obs_precision):
    level_count, row_count, col_count = control.shape
    lat_count = lax.axis_size("lat")
    lat_pos = lax.axis_index("lat")
    total_rows = row_count * lat_count
    row_ids = lat_pos * row_count + jnp.arange(row_count)
    lat_masked = kappa[1] * (row_ids < total_rows - 1).astype(jnp.float32)[:, None]
    coefficients = jnp.stack([kappa[0], lat_masked])

    def inside_rows(padded, margin):
        global_rows = lat_pos * row_count - margin + jnp.arange(row_count + 2 * margin)
        inside_mask = ((global_rows >= 0) & (global_rows < total_rows)).astype(jnp.float32)
        return padded * inside_mask[None, :, None]

    def rimmed(field_now):
        stacked = jnp.concatenate([field_now, coefficients], 0)
        padded = padded_2(stacked, (("lat", 1), ("lon", 2)), 1)
        padded = inside_rows(padded, 1)
        return (padded[:level_count], padded[level_count:])

    def smooth(field_now):
        for _ in range(STEPS):
            values_pad, coef_pad = rimmed(field_now)
            field_now = diffuse_step(values_pad, coef_pad)
        return field_now

    smoothed = smooth(control)
    state = jnp.dot(
        vert_sqrt,
        smoothed.reshape(level_count, -1),
        precision=lax.Precision.HIGHEST,
        preferred_element_type=jnp.float32,
    ).reshape(level_count, row_count, col_count)
    padded_state, _ = rimmed(state)
    flat_state = padded_state.reshape(level_count, -1)
    device_count = lat_count * lax.axis_size("lon")
    obs_count = obs_cell.shape[0]
    slot_cap = max(2, 2 * obs_count // device_count)
    tile_ids = obs_tile[:, 0]
    one_hot = (tile_ids[:, None] == jnp.arange(device_count)[None, :]).astype(jnp.int32)
    earlier = jnp.cumsum(one_hot, axis=0) - one_hot
    rank_within = jnp.sum(earlier * one_hot, axis=1)
    slot_index = tile_ids * slot_cap + rank_within
    payload = jnp.concatenate([obs_value, obs_precision, obs_frac], 0)
    send_values = (
        jnp.zeros((payload.shape[0], device_count * slot_cap), jnp.float32)
        .at[:, slot_index]
        .set(payload)
    )
    send_cells = (
        jnp.full((1, device_count * slot_cap), -1, jnp.int32).at[0, slot_index].set(obs_cell)
    )
    arrived, arrived_cells = (
        lax.all_to_all(send_values, ("lat", "lon"), split_axis=1, concat_axis=1, tiled=True),
        lax.all_to_all(send_cells, ("lat", "lon"), split_axis=1, concat_axis=1, tiled=True),
    )
    live_slot = (arrived_cells[0] >= 0).astype(jnp.float32)
    cell_ids = jnp.maximum(arrived_cells[0], 0)
    row_of = cell_ids // col_count
    col_of = cell_ids % col_count
    width_pad = col_count + 2
    base_index = (row_of + 1) * width_pad + col_of + 1
    east_frac = arrived[2 * level_count]
    north_frac = arrived[2 * level_count + 1]
    corners = [
        (base_index, (1.0 - east_frac) * (1.0 - north_frac)),
        (base_index + 1, east_frac * (1.0 - north_frac)),
        (base_index + width_pad, (1.0 - east_frac) * north_frac),
        (base_index + width_pad + 1, east_frac * north_frac),
    ]
    model_obs = jnp.zeros((level_count, cell_ids.shape[0]), jnp.float32)
    for corner_index, share in corners:
        model_obs = model_obs + share[None, :] * flat_state[:, corner_index]
    departure = (model_obs - arrived[:level_count]) * live_slot[None, :]
    weighted = arrived[level_count : 2 * level_count] * departure
    adjoint = jnp.zeros_like(flat_state)
    for corner_index, share in corners:
        adjoint = adjoint.at[:, corner_index].add(share[None, :] * weighted)
    adjoint = adjoint.reshape(level_count, row_count + 2, col_count + 2)
    adjoint_core = adjoint[:, 1:, 1:]
    east_column = adjoint_core[:, :, col_count]
    from_west = from_behind(east_column, "lon", 1)
    adjoint_core = adjoint_core[:, :, :col_count].at[:, :, 0].add(from_west)
    north_row = adjoint_core[:, row_count, :]
    from_south = from_behind_2(north_row, "lat", 1)
    adjoint_core = adjoint_core[:, :row_count].at[:, 0].add(from_south)
    back = jnp.dot(
        vert_sqrt.T,
        adjoint_core.reshape(level_count, -1),
        precision=lax.Precision.HIGHEST,
        preferred_element_type=jnp.float32,
    ).reshape(level_count, row_count, col_count)
    return control + smooth(back)


def solution(mesh):
    in_specs = (
        P(None, "lat", "lon"),
        P(None, "lat", "lon"),
        P(),
        P(("lat", "lon"), None),
        P(("lat", "lon")),
        P(None, ("lat", "lon")),
        P(None, ("lat", "lon")),
        P(None, ("lat", "lon")),
    )
    out_specs = P(None, "lat", "lon")
    return jax.shard_map(
        per_device, mesh=mesh, in_specs=in_specs, out_specs=out_specs, check_vma=False
    )
```

profile of v0, /device:TPU:0, one launch (start us, length us, event | category | flops | bytes accessed | tf_op | source)
XLA Modules:
  0.0 447.1 jit_solution(16061308345374079342)
XLA Ops:
  2.0 3.1 collective-permute-start
  5.1 2.1 collective-permute-start.1
  7.9 9.1 %reduce-window.6 = s32[32,16,128]{2,1,0:T(8,128)S(1)} reduce-window(s32[32,16,128]{2,1,0:T(8,128)S(1)} %fusion.158, s32[]{:T(128)} %constant.120.clone.1), window={size=1x1x128 pad=0_0x0_0x127_0}, to_apply=%region_0.0 | reduce-window | flops 8323072 | bytes 524292 | tf_op jit(solution)/shard_map/reduce-window
  18.1 8.8 %scatter_custom_fusion.5 = s32[4096]{0:T(1024)} fusion(s32[2048]{0:T(1024)S(1)} %broadcast_select_fusion, s32[2048]{0:T(1024)} %param.16, s32[]{:T(128)} %constant.118.clone.1), kind=kCustom, calls=%fused_computation.301 | custom fusion | bytes 16896
  26.9 4.2 all-to-all-start
  32.2 2.4 collective-permute-start.3
  34.7 4.0 collective-permute-done.2
  40.5 2.1 fusion.20
  44.9 2.4 collective-permute-start.5
  49.2 11.7 %scatter_custom_fusion = f32[130,4096]{0,1:T(8,128)} fusion(s32[2048]{0:T(1024)S(1)} %bitcast.152, f32[2048,130]{1,0:T(8,128)} %copy.85, f32[]{:T(128)} %constant.117.clone.1), kind=kCustom, calls=%fused_computation.78 | custom fusion | bytes 2130432 | tf_op jit(solution)/shard_map/scatter | solution.py:97
  60.8 5.0 %copy.86 = f32[130,32,128]{2,0,1:T(8,128)} copy(f32[130,32,128]{0,2,1:T(8,128)} %bitcast.138) | data formatting | bytes 4259840 | tf_op jit(solution)/shard_map/all_to_all | solution.py:103
  67.5 4.0 all-to-all-start.1
  74.3 2.4 fusion.25
  79.5 2.0 collective-permute-start.9
  81.5 31.8 %collective-permute-done.8 = f32[66,1,128]{2,1,0:T(1,128)S(1)} collective-permute-done((f32[66,1,128]{2,1,0:T(1,128)S(1)}, f32[66,1,128]{2,1,0:T(1,128)S(1)}, u32[]{:S(2)}, u32[]{:S(2)}) %collective-permute-start.8) | collective-permute-done | bytes 33824 | tf_op jit(solution)/shard_map/ppermute | solution.py:16
  119.3 4.0 collective-permute-done.10
  125.9 2.4 fusion.30
  129.2 11.7 %collective-permute-start.12 = (f32[66,1,128]{2,1,0:T(1,128)S(1)}, f32[66,1,128]{2,1,0:T(1,128)S(1)}, u32[]{:S(2)}, u32[]{:S(2)}) collective-permute-start(f32[66,1,128]{2,1,0:T(1,128)S(1)} %get-tuple-element.81), channel_id=1, source_target_pairs={{0,8},{8,16},{16,24},{24,0},{1,9},{9,17},{17,25},{25,1},{2,10},{10... | collective-permute-start | bytes 101384 | tf_op jit(solution)/shard_map/ppermute | solution.py:16
  142.5 2.3 collective-permute-done.13
  150.0 3.6 collective-permute-done.14
  156.2 2.4 fusion.35
  162.2 2.0 collective-permute-start.17
  164.2 2.1 collective-permute-done.16
  172.3 3.0 collective-permute-done.18
  177.9 3.5 fusion.62
  181.4 2.6 reshape.329
  185.5 14.1 %gather_fusion.3 = f32[4096,64]{1,0:T(8,128)} fusion(f32[64,2340]{0,1:T(8,128)S(1)} %copy.110, s32[4096]{0:T(1024)S(1)} %broadcast_clamp_fusion), kind=kCustom, calls=%fused_computation.3 | custom fusion | bytes 2113536 | tf_op jit(solution)/shard_map/gather | solution.py:122
  199.6 14.1 %gather_fusion.2 = f32[4096,64]{1,0:T(8,128)} fusion(f32[64,2340]{0,1:T(8,128)S(1)} %copy.110, s32[4096]{0:T(1024)S(1)} %broadcast_clamp_fusion.1), kind=kCustom, calls=%fused_computation.2 | custom fusion | bytes 2113536 | tf_op jit(solution)/shard_map/gather | solution.py:122
  213.6 14.1 %gather_fusion.1 = f32[4096,64]{1,0:T(8,128)} fusion(f32[64,2340]{0,1:T(8,128)S(1)} %copy.110, s32[4096]{0:T(1024)S(1)} %broadcast_clamp_fusion.2), kind=kCustom, calls=%fused_computation.1 | custom fusion | bytes 2113536 | tf_op jit(solution)/shard_map/gather | solution.py:122
  227.7 14.1 %gather_fusion = f32[4096,64]{1,0:T(8,128)} fusion(f32[64,2340]{0,1:T(8,128)S(1)} %copy.110, s32[4096]{0:T(1024)S(1)} %broadcast_clamp_fusion.3), kind=kCustom, calls=%fused_computation | custom fusion | bytes 2113536 | tf_op jit(solution)/shard_map/gather | solution.py:122
  243.1 3.2 copy.89
  246.3 2.1 copy.114
  248.4 7.9 %fusion.9 = f32[64,4096]{0,1:T(8,128)S(1)} fusion(f32[64,32,128]{0,2,1:T(8,128)} %copy.114, f32[64,32,128]{0,2,1:T(8,128)} %copy.89, f32[4096,64]{1,0:T(8,128)} %gather_fusion.3, f32[4096,64]{1,0:T(8,128)} %gather_fusion.2, f32[4096,64]{1,0:T(8,128)} %gather_fusion.1, f32[4096,64]{1,0:T(8,128)} %gather_fusion, f32[4096]{0:T(1024)S(1)} %get-tuple-element.91, ...), kind=kLoop, calls=%fused_computation.73 | loop fusion | flops 2621440 | bytes 7421952 | tf_op jit(solution)/shard_map/mul | solution.py:124
  256.3 28.4 %scatter_custom_fusion.1 = f32[64,2340]{0,1:T(8,128)S(1)} fusion(s32[4096]{0:T(1024)} %bitcast.162, f32[64,4096]{0,1:T(8,128)S(1)} %fusion.9, f32[4096]{0:T(1024)S(1)} %get-tuple-element.89, f32[]{:T(128)} %constant.117.clone.1), kind=kCustom, calls=%fused_computation.69 | custom fusion | flops 524288 | bytes 1664512 | tf_op jit(solution)/shard_map/scatter-add | solution.py:127
  284.7 28.5 %scatter_custom_fusion.2 = f32[64,2340]{0,1:T(8,128)S(1)} fusion(f32[64,2340]{0,1:T(8,128)S(1)} %scatter_custom_fusion.1, s32[4096]{0:T(1024)} %bitcast.154, f32[64,4096]{0,1:T(8,128)S(1)} %fusion.9, f32[4096]{0:T(1024)S(1)} %get-tuple-element.90), kind=kCustom, calls=%fused_computation.67 | custom fusion | flops 524288 | bytes 2712576 | tf_op jit(solution)/shard_map/scatter-add | solution.py:127
  313.2 28.5 %scatter_custom_fusion.3 = f32[64,2340]{0,1:T(8,128)S(1)} fusion(f32[64,2340]{0,1:T(8,128)S(1)} %scatter_custom_fusion.2, s32[4096]{0:T(1024)} %bitcast.160, f32[64,4096]{0,1:T(8,128)S(1)} %fusion.9, f32[4096]{0:T(1024)S(1)} %get-tuple-element.92), kind=kCustom, calls=%fused_computation.65 | custom fusion | flops 524288 | bytes 2712576 | tf_op jit(solution)/shard_map/scatter-add | solution.py:127
  341.8 28.8 %scatter_custom_fusion.4 = f32[64,2340]{0,1:T(8,128)S(1)} fusion(f32[64,2340]{0,1:T(8,128)S(1)} %scatter_custom_fusion.3, s32[4096]{0:T(1024)} %bitcast.158, f32[64,4096]{0,1:T(8,128)S(1)} %fusion.9, f32[4096]{0:T(1024)S(1)} %get-tuple-element.91), kind=kCustom, calls=%fused_computation.63 | custom fusion | flops 524288 | bytes 2712576 | tf_op jit(solution)/shard_map/scatter-add | solution.py:127
  375.5 2.8 collective-permute-done.20
  378.9 3.2 scatter-add.42
  387.2 2.4 collective-permute-start.22
  389.5 6.5 %collective-permute-start.23 = (f32[66,1,128]{2,1,0:T(1,128)S(1)}, f32[66,1,128]{2,1,0:T(1,128)S(1)}, u32[]{:S(2)}, u32[]{:S(2)}) collective-permute-start(f32[66,1,128]{2,1,0:T(1,128)S(1)} %get-tuple-element.78), channel_id=1, source_target_pairs={{8,0},{16,8},{24,16},{0,24},{9,1},{17,9},{25,17},{1,25},{10,2},{18... | collective-permute-start | bytes 101384 | tf_op jit(solution)/shard_map/ppermute | solution.py:18
  399.1 2.7 collective-permute-start.25
  406.7 2.8 collective-permute-start.27
  412.5 2.9 collective-permute-start.29
  420.4 2.7 collective-permute-start.31
  426.1 2.7 collective-permute-start.33
  433.8 2.7 collective-permute-start.35
  439.5 2.7 collective-permute-start.37
  (230 shorter events, 93.6 us)
Async XLA Ops:
  0.0 159.3 %copy-start = (f32[64,64]{1,0:T(8,128)S(1)}, f32[64,64]{1,0:T(8,128)}, u32[]{:S(2)}) copy-start(f32[64,64]{1,0:T(8,128)} %param.14) | copy-start | bytes 49156
  0.8 17.0 %copy-start.13 = (s32[2]{0:T(128)S(1)}, s32[2]{0:T(128)}, u32[]{:S(2)}) copy-start(s32[2]{0:T(128)} %constant.143) | copy-start | bytes 28
  0.8 17.1 %copy-start.12 = (s32[2]{0:T(128)S(1)}, s32[2]{0:T(128)}, u32[]{:S(2)}) copy-start(s32[2]{0:T(128)} %constant.140) | copy-start | bytes 28
  1.9 29.2 %copy-start.1 = (f32[64,16,128]{2,1,0:T(8,128)S(1)}, f32[64,16,128]{2,1,0:T(8,128)}, u32[]{:S(2)}) copy-start(f32[64,16,128]{2,1,0:T(8,128)} %param.12) | copy-start | bytes 1572868
  2.0 29.1 %collective-permute-start = (f32[66,1,128]{2,1,0:T(1,128)S(1)}, f32[66,1,128]{2,1,0:T(1,128)S(1)}, u32[]{:S(2)}, u32[]{:S(2)}) collective-permute-start(f32[66,1,128]{2,1,0:T(1,128)S(1)} %get-tuple-element.87), channel_id=1, source_target_pairs={{0,8},{8,16},{16,24},{24,0},{1,9},{9,17},{17,25},{25,1},{2,10},{10... | collective-permute-start | bytes 101384 | tf_op jit(solution)/shard_map/ppermute | solution.py:16
  5.1 26.0 %collective-permute-start.1 = (f32[66,1,128]{2,1,0:T(1,128)S(1)}, f32[66,1,128]{2,1,0:T(1,128)S(1)}, u32[]{:S(2)}, u32[]{:S(2)}) collective-permute-start(f32[66,1,128]{2,1,0:T(1,128)S(1)} %get-tuple-element.88), channel_id=1, source_target_pairs={{8,0},{16,8},{24,16},{0,24},{9,1},{17,9},{25,17},{1,25},{10,2},{18... | collective-permute-start | bytes 101384 | tf_op jit(solution)/shard_map/ppermute | solution.py:18
  26.9 40.6 %all-to-all-start = ((s32[1,32,128]{2,0,1:T(1,128)}), s32[1,32,128]{2,0,1:T(1,128)S(1)}, u32[]{:S(2)}, u32[]{:S(2)}) async-start(s32[1,32,128]{2,0,1:T(1,128)} %bitcast.6), calls=%async_computation | async-start | bytes 32768 | tf_op jit(solution)/shard_map/all_to_all | solution.py:104
  32.2 6.9 %collective-permute-start.3 = (f32[66,18,1]{0,1,2:T(8,128)S(1)}, f32[66,18,1]{0,1,2:T(8,128)S(1)}, u32[]{:S(2)}, u32[]{:S(2)}) collective-permute-start(f32[66,18,1]{0,1,2:T(8,128)S(1)} %copy.91), channel_id=1, source_target_pairs={{1,0},{2,1},{3,2},{4,3},{5,4},{6,5},{7,6},{0,7},{9,8},{10,9},{11,1... | collective-permute-start | bytes 14264 | tf_op jit(solution)/shard_map/ppermute | solution.py:18
  34.7 4.0 collective-permute-start.2
  43.4 22.4 %collective-permute-start.4 = (f32[66,1,128]{2,1,0:T(1,128)S(1)}, f32[66,1,128]{2,1,0:T(1,128)S(1)}, u32[]{:S(2)}, u32[]{:S(2)}) collective-permute-start(f32[66,1,128]{2,1,0:T(1,128)S(1)} %get-tuple-element.85), channel_id=1, source_target_pairs={{0,8},{8,16},{16,24},{24,0},{1,9},{9,17},{17,25},{25,1},{2,10},{10... | collective-permute-start | bytes 101384 | tf_op jit(solution)/shard_map/ppermute | solution.py:16
  44.9 20.9 %collective-permute-start.5 = (f32[66,1,128]{2,1,0:T(1,128)S(1)}, f32[66,1,128]{2,1,0:T(1,128)S(1)}, u32[]{:S(2)}, u32[]{:S(2)}) collective-permute-start(f32[66,1,128]{2,1,0:T(1,128)S(1)} %get-tuple-element.86), channel_id=1, source_target_pairs={{8,0},{16,8},{24,16},{0,24},{9,1},{17,9},{25,17},{1,25},{10,2},{18... | collective-permute-start | bytes 101384 | tf_op jit(solution)/shard_map/ppermute | solution.py:18
  66.9 6.0 %collective-permute-start.7 = (f32[66,18,1]{0,1,2:T(8,128)S(1)}, f32[66,18,1]{0,1,2:T(8,128)S(1)}, u32[]{:S(2)}, u32[]{:S(2)}) collective-permute-start(f32[66,18,1]{0,1,2:T(8,128)S(1)} %copy.95), channel_id=1, source_target_pairs={{1,0},{2,1},{3,2},{4,3},{5,4},{6,5},{7,6},{0,7},{9,8},{10,9},{11,1... | collective-permute-start | bytes 14264 | tf_op jit(solution)/shard_map/ppermute | solution.py:18
  67.0 4.7 %collective-permute-start.6 = (f32[66,18,1]{0,1,2:T(8,128)S(1)}, f32[66,18,1]{0,1,2:T(8,128)S(1)}, u32[]{:S(2)}, u32[]{:S(2)}) collective-permute-start(f32[66,18,1]{0,1,2:T(8,128)S(1)} %copy.94), channel_id=1, source_target_pairs={{0,1},{1,2},{2,3},{3,4},{4,5},{5,6},{6,7},{7,0},{8,9},{9,10},{10,1... | collective-permute-start | bytes 14264 | tf_op jit(solution)/shard_map/ppermute | solution.py:16
  67.5 174.3 %all-to-all-start.1 = ((f32[130,32,128]{2,0,1:T(8,128)}), f32[130,32,128]{2,0,1:T(8,128)S(1)}, u32[]{:S(2)}, u32[]{:S(2)}) async-start(f32[130,32,128]{2,0,1:T(8,128)} %copy.86), calls=%async_computation.1 | async-start | bytes 4456448 | tf_op jit(solution)/shard_map/all_to_all | solution.py:103
  71.7 47.6 %copy-start.6 = (s32[4096,1]{0,1:T(1,128)}, s32[4096,1]{0,1:T(1,128)S(1)}, u32[]{:S(2)}) copy-start(s32[4096,1]{0,1:T(1,128)S(1)} %get-tuple-element.29) | copy-start | bytes 49156
  77.6 35.8 %collective-permute-start.8 = (f32[66,1,128]{2,1,0:T(1,128)S(1)}, f32[66,1,128]{2,1,0:T(1,128)S(1)}, u32[]{:S(2)}, u32[]{:S(2)}) collective-permute-start(f32[66,1,128]{2,1,0:T(1,128)S(1)} %get-tuple-element.83), channel_id=1, source_target_pairs={{0,8},{8,16},{16,24},{24,0},{1,9},{9,17},{17,25},{25,1},{2,10},{10... | collective-permute-start | bytes 101384 | tf_op jit(solution)/shard_map/ppermute | solution.py:16
  79.5 33.8 %collective-permute-start.9 = (f32[66,1,128]{2,1,0:T(1,128)S(1)}, f32[66,1,128]{2,1,0:T(1,128)S(1)}, u32[]{:S(2)}, u32[]{:S(2)}) collective-permute-start(f32[66,1,128]{2,1,0:T(1,128)S(1)} %get-tuple-element.84), channel_id=1, source_target_pairs={{8,0},{16,8},{24,16},{0,24},{9,1},{17,9},{25,17},{1,25},{10,2},{18... | collective-permute-start | bytes 101384 | tf_op jit(solution)/shard_map/ppermute | solution.py:18
  81.5 59.4 %copy-start.9 = (s32[4096,1]{0,1:T(1,128)}, s32[4096,1]{0,1:T(1,128)S(1)}, u32[]{:S(2)}) copy-start(s32[4096,1]{0,1:T(1,128)S(1)} %get-tuple-element.126) | copy-start | bytes 49156
  81.5 68.4 %copy-start.8 = (s32[4096,1]{0,1:T(1,128)}, s32[4096,1]{0,1:T(1,128)S(1)}, u32[]{:S(2)}) copy-start(s32[4096,1]{0,1:T(1,128)S(1)} %get-tuple-element.125) | copy-start | bytes 49156
  81.5 82.6 %copy-start.7 = (s32[4096,1]{0,1:T(1,128)}, s32[4096,1]{0,1:T(1,128)S(1)}, u32[]{:S(2)}) copy-start(s32[4096,1]{0,1:T(1,128)S(1)} %get-tuple-element.127) | copy-start | bytes 49156
  117.9 6.7 %collective-permute-start.11 = (f32[66,18,1]{0,1,2:T(8,128)S(1)}, f32[66,18,1]{0,1,2:T(8,128)S(1)}, u32[]{:S(2)}, u32[]{:S(2)}) collective-permute-start(f32[66,18,1]{0,1,2:T(8,128)S(1)} %copy.99), channel_id=1, source_target_pairs={{1,0},{2,1},{3,2},{4,3},{5,4},{6,5},{7,6},{0,7},{9,8},{10,9},{11,1... | collective-permute-start | bytes 14264 | tf_op jit(solution)/shard_map/ppermute | solution.py:18
  119.3 4.0 collective-permute-start.10
  129.2 13.4 %collective-permute-start.12 = (f32[66,1,128]{2,1,0:T(1,128)S(1)}, f32[66,1,128]{2,1,0:T(1,128)S(1)}, u32[]{:S(2)}, u32[]{:S(2)}) collective-permute-start(f32[66,1,128]{2,1,0:T(1,128)S(1)} %get-tuple-element.81), channel_id=1, source_target_pairs={{0,8},{8,16},{16,24},{24,0},{1,9},{9,17},{17,25},{25,1},{2,10},{10... | collective-permute-start | bytes 101384 | tf_op jit(solution)/shard_map/ppermute | solution.py:16
  140.9 3.9 collective-permute-start.13
  149.4 5.4 %collective-permute-start.15 = (f32[66,18,1]{0,1,2:T(8,128)S(1)}, f32[66,18,1]{0,1,2:T(8,128)S(1)}, u32[]{:S(2)}, u32[]{:S(2)}) collective-permute-start(f32[66,18,1]{0,1,2:T(8,128)S(1)} %copy.103), channel_id=1, source_target_pairs={{1,0},{2,1},{3,2},{4,3},{5,4},{6,5},{7,6},{0,7},{9,8},{10,9},{11,1... | collective-permute-start | bytes 14264 | tf_op jit(solution)/shard_map/ppermute | solution.py:18
  149.4 4.1 collective-permute-start.14
  160.3 6.0 %collective-permute-start.16 = (f32[66,1,128]{2,1,0:T(1,128)S(1)}, f32[66,1,128]{2,1,0:T(1,128)S(1)}, u32[]{:S(2)}, u32[]{:S(2)}) collective-permute-start(f32[66,1,128]{2,1,0:T(1,128)S(1)} %get-tuple-element.79), channel_id=1, source_target_pairs={{0,8},{8,16},{16,24},{24,0},{1,9},{9,17},{17,25},{25,1},{2,10},{10... | collective-permute-start | bytes 101384 | tf_op jit(solution)/shard_map/ppermute | solution.py:16
  162.2 4.3 collective-permute-start.17
  171.0 5.6 %collective-permute-start.19 = (f32[66,18,1]{0,1,2:T(8,128)S(1)}, f32[66,18,1]{0,1,2:T(8,128)S(1)}, u32[]{:S(2)}, u32[]{:S(2)}) collective-permute-start(f32[66,18,1]{0,1,2:T(8,128)S(1)} %copy.107), channel_id=1, source_target_pairs={{1,0},{2,1},{3,2},{4,3},{5,4},{6,5},{7,6},{0,7},{9,8},{10,9},{11,1... | collective-permute-start | bytes 14264 | tf_op jit(solution)/shard_map/ppermute | solution.py:18
  171.0 4.2 collective-permute-start.18
  374.2 4.0 collective-permute-start.20
  383.2 2.9 collective-permute-start.21
  387.2 10.8 %collective-permute-start.22 = (f32[66,1,128]{2,1,0:T(1,128)S(1)}, f32[66,1,128]{2,1,0:T(1,128)S(1)}, u32[]{:S(2)}, u32[]{:S(2)}) collective-permute-start(f32[66,1,128]{2,1,0:T(1,128)S(1)} %get-tuple-element.77), channel_id=1, source_target_pairs={{0,8},{8,16},{16,24},{24,0},{1,9},{9,17},{17,25},{25,1},{2,10},{10... | collective-permute-start | bytes 101384 | tf_op jit(solution)/shard_map/ppermute | solution.py:16
  389.5 8.4 %collective-permute-start.23 = (f32[66,1,128]{2,1,0:T(1,128)S(1)}, f32[66,1,128]{2,1,0:T(1,128)S(1)}, u32[]{:S(2)}, u32[]{:S(2)}) collective-permute-start(f32[66,1,128]{2,1,0:T(1,128)S(1)} %get-tuple-element.78), channel_id=1, source_target_pairs={{8,0},{16,8},{24,16},{0,24},{9,1},{17,9},{25,17},{1,25},{10,2},{18... | collective-permute-start | bytes 101384 | tf_op jit(solution)/shard_map/ppermute | solution.py:18
  398.7 4.0 collective-permute-start.24
  399.1 4.1 collective-permute-start.25
  405.5 5.8 %collective-permute-start.26 = (f32[66,1,128]{2,1,0:T(1,128)S(1)}, f32[66,1,128]{2,1,0:T(1,128)S(1)}, u32[]{:S(2)}, u32[]{:S(2)}) collective-permute-start(f32[66,1,128]{2,1,0:T(1,128)S(1)} %get-tuple-element.75), channel_id=1, source_target_pairs={{0,8},{8,16},{16,24},{24,0},{1,9},{9,17},{17,25},{25,1},{2,10},{10... | collective-permute-start | bytes 101384 | tf_op jit(solution)/shard_map/ppermute | solution.py:16
  406.7 4.7 %collective-permute-start.27 = (f32[66,1,128]{2,1,0:T(1,128)S(1)}, f32[66,1,128]{2,1,0:T(1,128)S(1)}, u32[]{:S(2)}, u32[]{:S(2)}) collective-permute-start(f32[66,1,128]{2,1,0:T(1,128)S(1)} %get-tuple-element.76), channel_id=1, source_target_pairs={{8,0},{16,8},{24,16},{0,24},{9,1},{17,9},{25,17},{1,25},{10,2},{18... | collective-permute-start | bytes 101384 | tf_op jit(solution)/shard_map/ppermute | solution.py:18
  412.1 4.0 collective-permute-start.28
  412.5 4.3 collective-permute-start.29
  419.1 5.8 %collective-permute-start.30 = (f32[66,1,128]{2,1,0:T(1,128)S(1)}, f32[66,1,128]{2,1,0:T(1,128)S(1)}, u32[]{:S(2)}, u32[]{:S(2)}) collective-permute-start(f32[66,1,128]{2,1,0:T(1,128)S(1)} %get-tuple-element.73), channel_id=1, source_target_pairs={{0,8},{8,16},{16,24},{24,0},{1,9},{9,17},{17,25},{25,1},{2,10},{10... | collective-permute-start | bytes 101384 | tf_op jit(solution)/shard_map/ppermute | solution.py:16
  420.4 4.5 %collective-permute-start.31 = (f32[66,1,128]{2,1,0:T(1,128)S(1)}, f32[66,1,128]{2,1,0:T(1,128)S(1)}, u32[]{:S(2)}, u32[]{:S(2)}) collective-permute-start(f32[66,1,128]{2,1,0:T(1,128)S(1)} %get-tuple-element.74), channel_id=1, source_target_pairs={{8,0},{16,8},{24,16},{0,24},{9,1},{17,9},{25,17},{1,25},{10,2},{18... | collective-permute-start | bytes 101384 | tf_op jit(solution)/shard_map/ppermute | solution.py:18
  425.7 4.0 collective-permute-start.32
  426.1 4.1 collective-permute-start.33
  432.5 5.9 %collective-permute-start.34 = (f32[66,1,128]{2,1,0:T(1,128)S(1)}, f32[66,1,128]{2,1,0:T(1,128)S(1)}, u32[]{:S(2)}, u32[]{:S(2)}) collective-permute-start(f32[66,1,128]{2,1,0:T(1,128)S(1)} %get-tuple-element.71), channel_id=1, source_target_pairs={{0,8},{8,16},{16,24},{24,0},{1,9},{9,17},{17,25},{25,1},{2,10},{10... | collective-permute-start | bytes 101384 | tf_op jit(solution)/shard_map/ppermute | solution.py:16
  433.8 4.5 %collective-permute-start.35 = (f32[66,1,128]{2,1,0:T(1,128)S(1)}, f32[66,1,128]{2,1,0:T(1,128)S(1)}, u32[]{:S(2)}, u32[]{:S(2)}) collective-permute-start(f32[66,1,128]{2,1,0:T(1,128)S(1)} %get-tuple-element.72), channel_id=1, source_target_pairs={{8,0},{16,8},{24,16},{0,24},{9,1},{17,9},{25,17},{1,25},{10,2},{18... | collective-permute-start | bytes 101384 | tf_op jit(solution)/shard_map/ppermute | solution.py:18
  439.1 4.0 collective-permute-start.36
  439.5 4.1 collective-permute-start.37
  (6 other events, 34.0 us)
where the time goes:
time: 455 us; the launch traced here: 447 us
  other arithmetic  160 us (35%)
  local copies, waits for them, and re-layouts  142 us (31%)
  starting transfers between devices  75.6 us (17%)
  waiting for transfers between devices  67.2 us (15%)
    scatter-add x4, other arithmetic, per_device(): adjoint = adjoint.at[:, corner_index].add(share[None, :] * weighted)  114 us
    ppermute x18, waiting for transfers between devices, padded_2(): lax.ppermute(tail, axis, [(i, (i + 1) % count) for i in range(count)])  61.1 us
    gather x4, local copies, waits for them, and re-layouts, per_device(): model_obs = model_obs + share[None, :] * flat_state[:, corner_index]  56.4 us
    ppermute x18, starting transfers between devices, padded_2(): lax.ppermute(head, axis, [((i + 1) % count, i) for i in range(count)])  37.9 us
    ppermute x18, starting transfers between devices, padded_2(): lax.ppermute(tail, axis, [(i, (i + 1) % count) for i in range(count)])  28.1 us
    mul x9, other arithmetic, inside_rows(): return padded * inside_mask[None, :, None]  16.8 us
    slice x27, local copies, waits for them, and re-layouts, padded_2(): lax.slice_in_dim(cells, cells.shape[dim] - width, cells.shape[dim], axis=...  13 us
    scatter x1, local copies, waits for them, and re-layouts, per_device(): send_values = jnp.zeros((payload.shape[0], device_count * slot_cap), jnp....  11.7 us
  transfers between devices with their start and end apart: 40, of which 20 were waited for; matrix products, arithmetic and copies ran while one was open for 33% of the time, Pallas kernels for 0%

commit v1 on v0

v1 whole, which is shorter than its diff:
```python
import functools

import jax
import jax.numpy as jnp
from jax import lax
from jax.experimental import pallas as pl
from jax.experimental.pallas import tpu as pltpu
from jax.sharding import PartitionSpec as P

STEPS = 4
ROWS_SENT = 136
MESH = pl.DeviceIdType.MESH
SIDES = ((0, 1), (0, -1), (1, 1), (1, -1), (-1, 1), (-1, -1))
NT = (((1,), (1,)), ((), ()))
BF = jnp.bfloat16
F32 = jnp.float32


def split_two(x):
    hi = x.astype(BF)
    return hi, (x - hi.astype(F32)).astype(BF)


def pack_kernel(tiles, cap, tile_ref, cell_ref, frac_ref, value_ref, prec_ref, out_ref, pay_ref, slot_ref):
    lev, count = value_ref.shape
    tile = tile_ref[...]
    named = (lax.broadcasted_iota(jnp.int32, (tiles, count), 0) == tile).astype(F32)
    width = 256
    upper = (
        lax.broadcasted_iota(jnp.int32, (width, width), 0)
        < lax.broadcasted_iota(jnp.int32, (width, width), 1)
    ).astype(F32).astype(BF)
    carry = jnp.zeros((tiles, 1), F32)
    for first in range(0, count, width):
        part = named[:, first : first + width]
        before = jnp.dot(part.astype(BF), upper, preferred_element_type=F32) + carry
        rank = jnp.sum(before * part, axis=0, keepdims=True)
        slot_ref[:, first : first + width] = (
            tile[:, first : first + width] * cap + rank.astype(jnp.int32)
        )
        carry = carry + jnp.sum(part, axis=1, keepdims=True)
    tail = jnp.concatenate(
        [frac_ref[...], cell_ref[...].astype(F32), jnp.zeros((13, count), F32)], 0
    )
    at = 0
    for piece in (value_ref[...], prec_ref[...], tail):
        hi, lo = split_two(piece)
        n = piece.shape[0]
        pay_ref[at : at + n, :] = hi
        pay_ref[144 + at : 144 + at + n, :] = lo
        at += n
    group = 256 // cap
    slots = slot_ref[...]

    def body(g, _):
        ids = lax.broadcasted_iota(jnp.int32, (256, count), 0) + g * 256
        hot = (ids == slots).astype(F32).astype(BF)
        got = lax.dot_general(pay_ref[...], hot, NT, preferred_element_type=F32)
        both = got[:ROWS_SENT] + got[144 : 144 + ROWS_SENT]
        for j in range(group):
            out_ref[g * group + j] = both[:, j * cap : (j + 1) * cap]
        return 0

    lax.fori_loop(0, tiles // group, body, 0)


def main_kernel(
    n_lat, n_lon, send_ref, control_ref, kappa_ref, vert_ref, vert_t_ref, out_ref,
    recv, ext, side, edges, near, coef, wide, s4, a4, row_out, row_in, col_out, col_in,
    ext2, side2, edges2, near2,
    a_send, a_recv, own_sem, lat_send, lat_recv, lon_send, lon_recv, st_send, st_recv,
    ad_send, ad_recv, lat2_send, lat2_recv, lon2_send, lon2_recv,
):
    devices, _, cap = recv.shape
    lev, rows, cols = control_ref.shape
    lat, lon = lax.axis_index("lat"), lax.axis_index("lon")
    me = lat * n_lon + lon
    top = lat == n_lat - 1
    bottom = lat == 0

    def to(dy, dx):
        return (lax.rem(lat + dy + n_lat, n_lat), lax.rem(lon + dx + n_lon, n_lon))

    def at_distance(k):
        d = lax.rem(me + k, devices)
        return d // n_lon, lax.rem(d, n_lon), d

    barrier = pltpu.get_barrier_semaphore()

    def greet(k, _):
        y, x, _d = at_distance(k)
        pl.semaphore_signal(barrier, inc=1, device_id=(y, x), device_id_type=MESH)
        return 0

    lax.fori_loop(1, devices, greet, 0)
    pl.semaphore_wait(barrier, devices - 1)

    def obs_copy(k):
        y, x, d = at_distance(k)
        return pltpu.make_async_remote_copy(
            src_ref=send_ref.at[d], dst_ref=recv.at[k], send_sem=a_send.at[k],
            recv_sem=a_recv.at[k], device_id=(y, x), device_id_type=MESH,
        )

    lane = lax.broadcasted_iota(jnp.int32, (1, cols), 1)

    def edge_block(values):
        acc = jnp.zeros(values[0].shape, F32)
        for r, x in enumerate(values):
            acc = jnp.where((lane >= 4 * r) & (lane < 4 * r + 4), pltpu.roll(x, (4 * r + 4) % cols, 1), acc)
            b = 64 + 4 * r
            acc = jnp.where((lane >= b) & (lane < b + 4), pltpu.roll(x, b % cols, 1), acc)
        return acc

    def halo_copies(ext_, edges_, near_, sems):
        ls, lr, os, orr = sems
        copies = [
            pltpu.make_async_remote_copy(
                src_ref=ext_.at[pl.ds(4, 4)], dst_ref=ext_.at[pl.ds(rows + 4, 4)], send_sem=ls.at[0],
                recv_sem=lr.at[0], device_id=to(-1, 0), device_id_type=MESH),
            pltpu.make_async_remote_copy(
                src_ref=ext_.at[pl.ds(rows, 4)], dst_ref=ext_.at[pl.ds(0, 4)], send_sem=ls.at[1],
                recv_sem=lr.at[1], device_id=to(1, 0), device_id_type=MESH),
        ]
        for j, (dy, dx) in enumerate(SIDES):
            copies.append(pltpu.make_async_remote_copy(
                src_ref=edges_, dst_ref=near_.at[j], send_sem=os.at[j], recv_sem=orr.at[j],
                device_id=to(-dy, -dx), device_id_type=MESH))
        return copies

    def build_side(near_, side_):
        for r in range(rows + 8):
            q = r - 4
            dy = 0 if 0 <= q < rows else (-1 if q < 0 else 1)
            rr = q - dy * rows
            east = near_[SIDES.index((dy, 1))]
            west = near_[SIDES.index((dy, -1))]
            side_[r] = jnp.where(
                lane < 4, pltpu.roll(east, (cols - 64 - 4 * rr) % cols, 1),
                jnp.where(lane >= cols - 4, pltpu.roll(west, (cols - 4 - 4 * rr) % cols, 1), 0.0))

    def ring(m, s, step):
        shift = 1 if step < 0 else cols - 1
        edge = lane == (0 if step < 0 else cols - 1)
        rm, rs = pltpu.roll(m, shift, 1), pltpu.roll(s, shift, 1)
        return jnp.where(edge, rs, rm), jnp.where(edge, rm, rs)

    def smooth(main_, side_, put):
        def body(b, _):
            lv = pl.ds(pl.multiple_of(b * 8, 8), 8)
            m = [main_[r, lv, :] for r in range(rows + 8)]
            s = [side_[r, lv, :] for r in range(rows + 8)]
            for step in range(STEPS):
                nm, ns = list(m), list(s)
                for r in range(step + 1, rows + 7 - step):
                    em, es = ring(m[r], s[r], 1)
                    wm, ws = ring(m[r], s[r], -1)
                    nm[r] = (coef[0, r] * m[r] + coef[1, r] * em + coef[2, r] * wm
                             + coef[3, r] * m[r + 1] + coef[3, r - 1] * m[r - 1])
                    if step < STEPS - 1:
                        ns[r] = (coef[4, r] * s[r] + coef[5, r] * es + coef[6, r] * ws
                                 + coef[7, r] * s[r + 1] + coef[7, r - 1] * s[r - 1])
                m, s = nm, ns
            for r in range(rows):
                put(lv, r, m[r + 4])
            return 0

        lax.fori_loop(0, lev // 8, body, 0)

    zero6 = jnp.zeros((6, cols), F32)
    for r in range(rows):
        ext[r + 4, 0:lev, :] = control_ref[:, r, :]
        north = kappa_ref[1, r : r + 1, :]
        if r == rows - 1:
            north = jnp.where(top, 0.0, north)
        ext[r + 4, lev : lev + 8, :] = jnp.concatenate([kappa_ref[0, r : r + 1, :], north, zero6], 0)
    edges[...] = edge_block([ext[r + 4] for r in range(rows)])
    first = halo_copies(ext, edges, near, (lat_send, lat_recv, lon_send, lon_recv))
    for c in first:
        c.start()

    def start_obs(k, _):
        obs_copy(k).start()
        return 0

    lax.fori_loop(1, devices, start_obs, 0)
    own = pltpu.make_async_copy(send_ref.at[me], recv.at[0], own_sem)
    own.start()
    for c in first:
        c.wait()
    build_side(near, side)

    def spread(x):
        return jnp.broadcast_to(x, (8, cols))

    for r in range(rows + 8):
        km, ks = ext[r, lev : lev + 8, :], side[r, lev : lev + 8, :]
        em, es = spread(km[0:1]), spread(ks[0:1])
        wm, ws = ring(em, es, -1)
        nm, ns = spread(km[1:2]), spread(ks[1:2])
        coef[1, r], coef[2, r], coef[3, r] = em, wm, nm
        coef[5, r], coef[6, r], coef[7, r] = es, ws, ns
        if r:
            coef[0, r] = 1.0 - em - wm - nm - coef[3, r - 1]
            coef[4, r] = 1.0 - es - ws - ns - coef[7, r - 1]

    def put_wide(lv, r, x):
        wide[lv, r * cols : (r + 1) * cols] = x

    smooth(ext, side, put_wide)
    wide[...] = jnp.dot(vert_ref[...], wide[...], precision=lax.Precision.HIGHEST, preferred_element_type=F32)

    def row(r):
        return wide[:, r * cols : (r + 1) * cols]

    row_out[0] = row(0)
    acc = jnp.zeros((lev, cols), F32)
    for r in range(rows):
        acc = jnp.where(lane == r, pltpu.roll(row(r), r, 1), acc)
    col_out[0] = acc

    def trio(which, sign, sems, semr):
        return [
            pltpu.make_async_remote_copy(
                src_ref=row_out.at[which], dst_ref=row_in.at[which], send_sem=sems.at[0], recv_sem=semr.at[0],
                device_id=to(sign, 0), device_id_type=MESH),
            pltpu.make_async_remote_copy(
                src_ref=col_out.at[which], dst_ref=col_in.at[which, 0], send_sem=sems.at[1], recv_sem=semr.at[1],
                device_id=to(0, sign), device_id_type=MESH),
            pltpu.make_async_remote_copy(
                src_ref=col_out.at[which], dst_ref=col_in.at[which, 1], send_sem=sems.at[2], recv_sem=semr.at[2],
                device_id=to(sign, sign), device_id_type=MESH),
        ]

    second = trio(0, -1, st_send, st_recv)
    for c in second:
        c.start()
    for c in second:
        c.wait()
    last_row = jnp.where(top, 0.0, row_in[0])
    last_corner = jnp.where(top, 0.0, col_in[0, 1])

    def put_s4(corner, r, x):
        hi, lo = split_two(x)
        s4[corner * lev : (corner + 1) * lev, r * cols : (r + 1) * cols] = hi
        s4[(corner + 4) * lev : (corner + 5) * lev, r * cols : (r + 1) * cols] = lo

    for r in range(rows + 1):
        x = row(r) if r < rows else last_row
        over = pltpu.roll(col_in[0, 0], cols - 1 - r, 1) if r < rows else pltpu.roll(last_corner, cols - 1, 1)
        e = jnp.where(lane == cols - 1, over, pltpu.roll(x, cols - 1, 1))
        if r < rows:
            put_s4(0, r, x)
            put_s4(1, r, e)
        if r:
            put_s4(2, r - 1, x)
            put_s4(3, r - 1, e)

    a4[...] = jnp.zeros_like(a4)
    own.wait()
    group = max(1, 256 // cap)

    def work(g, _):
        for j in range(group):
            k = g * group + j

            @pl.when(k > 0)
            def _():
                obs_copy(k).wait_recv()

        got = jnp.concatenate([recv[g * group + j] for j in range(group)], 1)
        fx, fy = got[2 * lev : 2 * lev + 1], got[2 * lev + 1 : 2 * lev + 2]
        cell = got[2 * lev + 2 : 2 * lev + 3].astype(jnp.int32)
        hot = (lax.broadcasted_iota(jnp.int32, (rows * cols, group * cap), 0) == cell).astype(F32).astype(BF)
        m4 = jnp.dot(s4[...], hot, preferred_element_type=F32)
        shares = ((1.0 - fx) * (1.0 - fy), fx * (1.0 - fy), (1.0 - fx) * fy, fx * fy)
        model = jnp.zeros((lev, group * cap), F32)
        for c, w in enumerate(shares):
            model = model + w * (m4[c * lev : (c + 1) * lev] + m4[(c + 4) * lev : (c + 5) * lev])
        weighted = got[lev : 2 * lev] * (model - got[:lev])
        hi, lo = split_two(jnp.concatenate([w * weighted for w in shares], 0))
        a4[...] += (lax.dot_general(hi, hot, NT, preferred_element_type=F32)
                    + lax.dot_general(lo, hot, NT, preferred_element_type=F32))
        return 0

    lax.fori_loop(0, devices // group, work, 0)

    def part(c, r):
        return a4[c * lev : (c + 1) * lev, r * cols : (r + 1) * cols]

    here, above, packed = [], [], jnp.zeros((lev, cols), F32)
    for r in range(rows):
        e0, e1 = pltpu.roll(part(1, r), 1, 1), pltpu.roll(part(3, r), 1, 1)
        here.append(part(0, r) + jnp.where(lane == 0, 0.0, e0))
        above.append(part(2, r) + jnp.where(lane == 0, 0.0, e1))
        packed = packed + jnp.where(lane == r, pltpu.roll(e0, r, 1), 0.0)
        packed = packed + jnp.where(lane == r + 1, pltpu.roll(e1, r + 1, 1), 0.0)
        wide[:, r * cols : (r + 1) * cols] = here[r] + above[r - 1] if r else here[r]
    row_out[1] = above[rows - 1]
    col_out[1] = packed
    third = trio(1, 1, ad_send, ad_recv)
    for c in third:
        c.start()
    for c in third:
        c.wait()
    wide[:, 0:cols] += (jnp.where(bottom, 0.0, row_in[1])
                        + jnp.where((lane == 0) & jnp.logical_not(bottom), pltpu.roll(col_in[1, 1], cols - rows, 1), 0.0))
    for r in range(rows):
        wide[:, r * cols : (r + 1) * cols] += jnp.where(
            lane == 0, pltpu.roll(col_in[1, 0], (cols - r) % cols, 1), 0.0)
    back = jnp.dot(vert_t_ref[...], wide[...], precision=lax.Precision.HIGHEST, preferred_element_type=F32)
    for r in range(rows):
        ext2[r + 4] = back[:, r * cols : (r + 1) * cols]
    edges2[...] = edge_block([ext2[r + 4] for r in range(rows)])
    fourth = halo_copies(ext2, edges2, near2, (lat2_send, lat2_recv, lon2_send, lon2_recv))
    for c in fourth:
        c.start()
    for c in fourth:
        c.wait()
    build_side(near2, side2)

    def put_out(lv, r, x):
        out_ref[lv, r, :] = x

    smooth(ext2, side2, put_out)

    def end_obs(k, _):
        obs_copy(k).wait_send()
        return 0

    lax.fori_loop(1, devices, end_obs, 0)


def per_device(control, kappa, vert_sqrt, obs_tile, obs_cell, obs_frac, obs_value, obs_precision):
    lev, rows, cols = control.shape
    n_lat, n_lon = lax.axis_size("lat"), lax.axis_size("lon")
    devices = n_lat * n_lon
    count = obs_cell.shape[0]
    cap = 2 * count // devices
    vmem = pl.BlockSpec(memory_space=pltpu.VMEM)
    send = pl.pallas_call(
        functools.partial(pack_kernel, devices, cap),
        out_shape=jax.ShapeDtypeStruct((devices, ROWS_SENT, cap), F32),
        in_specs=[vmem] * 5,
        out_specs=vmem,
        scratch_shapes=[pltpu.VMEM((288, count), BF), pltpu.VMEM((1, count), jnp.int32)],
        compiler_params=pltpu.CompilerParams(vmem_limit_bytes=48 * 2**20),
        name="pack",
    )(obs_tile.reshape(1, count), obs_cell.reshape(1, count), obs_frac, obs_value, obs_precision)
    dma = pltpu.SemaphoreType.DMA
    smoothed = pl.pallas_call(
        functools.partial(main_kernel, n_lat, n_lon),
        out_shape=jax.ShapeDtypeStruct((lev, rows, cols), F32),
        in_specs=[pl.BlockSpec(memory_space=pl.ANY)] + [vmem] * 4,
        out_specs=vmem,
        scratch_shapes=[
            pltpu.VMEM((devices, ROWS_SENT, cap), F32),
            pltpu.VMEM((rows + 8, lev + 8, cols), F32),
            pltpu.VMEM((rows + 8, lev + 8, cols), F32),
            pltpu.VMEM((lev + 8, cols), F32),
            pltpu.VMEM((6, lev + 8, cols), F32),
            pltpu.VMEM((8, rows + 8, 8, cols), F32),
            pltpu.VMEM((lev, rows * cols), F32),
            pltpu.VMEM((8 * lev, rows * cols), BF),
            pltpu.VMEM((4 * lev, rows * cols), F32),
            pltpu.VMEM((2, lev, cols), F32),
            pltpu.VMEM((2, lev, cols), F32),
            pltpu.VMEM((2, lev, cols), F32),
            pltpu.VMEM((2, 2, lev, cols), F32),
            pltpu.VMEM((rows + 8, lev, cols), F32),
            pltpu.VMEM((rows + 8, lev, cols), F32),
            pltpu.VMEM((lev, cols), F32),
            pltpu.VMEM((6, lev, cols), F32),
            dma((devices,)), dma((devices,)), dma,
            dma((2,)), dma((2,)), dma((6,)), dma((6,)),
            dma((3,)), dma((3,)), dma((3,)), dma((3,)),
            dma((2,)), dma((2,)), dma((6,)), dma((6,)),
        ],
        compiler_params=pltpu.CompilerParams(
            collective_id=0, has_side_effects=True, vmem_limit_bytes=48 * 2**20),
        name="main",
    )(send, control, kappa, vert_sqrt, vert_sqrt.T)
    return control + smoothed


def solution(mesh):
    in_specs = (
        P(None, "lat", "lon"), P(None, "lat", "lon"), P(), P(("lat", "lon"), None), P(("lat", "lon")),
        P(None, ("lat", "lon")), P(None, ("lat", "lon")), P(None, ("lat", "lon")),
    )
    return jax.shard_map(
        per_device, mesh=mesh, in_specs=in_specs, out_specs=P(None, "lat", "lon"), check_vma=False
    )
```

time: 455 us -> 146 us (0.32); the launches traced: 447 us -> 145 us
  other arithmetic: 160 us -> 0.86 us
  Pallas kernels: 0 us -> 139 us
  local copies, waits for them, and re-layouts: 142 us -> 5.09 us
  starting transfers between devices: 75.6 us -> 0 us
  waiting for transfers between devices: 67.2 us -> 0 us
    pallas_call x0 -> x2, Pallas kernels: none -> 139 us  [the longest x1 131 us: per_device(): pl.pallas_call(functools.partial(main_kernel, n_lat, n_lon), out_shape=ja...]
    scatter-add x4 -> x0, other arithmetic: 114 us -> none  [per_device(): adjoint = adjoint.at[:, corner_index].add(share[None, :] * weighted)]
    ppermute x38 -> x0, starting transfers between devices: 67.4 us -> none  [the longest x18 37.9 us: padded_2(): lax.ppermute(head, axis, [((i + 1) % count, i) for i in range(count)])]
    ppermute x38 -> x0, waiting for transfers between devices: 67.2 us -> none  [the longest x18 61.1 us: padded_2(): lax.ppermute(tail, axis, [(i, (i + 1) % count) for i in range(count)])]
    gather x4 -> x0, local copies, waits for them, and re-layouts: 56.4 us -> none  [per_device(): model_obs = model_obs + share[None, :] * flat_state[:, corner_index]]
    slice x60 -> x0, local copies, waits for them, and re-layouts: 31.3 us -> none  [the longest x27 13 us: padded_2(): lax.slice_in_dim(cells, cells.shape[dim] - width, cells.shape[dim], axis=...]
    mul x11 -> x0, other arithmetic: 24.7 us -> none  [the longest x9 16.8 us: inside_rows(): return padded * inside_mask[None, :, None]]
    ppermute x18 -> x0, local copies, waits for them, and re-layouts: 15.5 us -> none  [the longest x9 8.27 us: padded_2(): lax.ppermute(head, axis, [((i + 1) % count, i) for i in range(count)])]
  transfers between devices with their start and end apart: 40 -> 0, of which waited for: 20 -> 0; matrix products, arithmetic and copies ran while one was open for 33% -> 0% of each run, Pallas kernels for 0% -> 0%
where the time goes in v1:
time: 146 us; the launch traced here: 145 us
  Pallas kernels  139 us (95%)
  local copies, waits for them, and re-layouts  5.09 us (3%)
    pallas_call x1, Pallas kernels, per_device(): pl.pallas_call(functools.partial(main_kernel, n_lat, n_lon), out_shape=ja...  131 us
    pallas_call x1, Pallas kernels, per_device(): pl.pallas_call(functools.partial(pack_kernel, devices, cap), out_shape=ja...  8.62 us
    unnamed x17, local copies, waits for them, and re-layouts  5.09 us

profile of v1, /device:TPU:0, one launch (start us, length us, event | category | flops | bytes accessed | tf_op | source)
XLA Modules:
  0.0 145.4 jit_solution(4847557646124484326)
XLA Ops:
  0.0 0.0 copy-start
  0.0 0.9 copy.9
  0.9 0.0 copy-start.1
  0.9 1.0 copy-done.1
  1.9 0.0 copy-start.2
  1.9 1.0 copy-done.2
  3.0 0.0 copy-start.4
  3.0 0.7 copy-done.4
  3.7 0.0 copy-start.6
  3.7 0.7 copy-done.6
  4.4 0.0 copy-start.7
  4.4 0.7 copy-done.7
  5.1 0.0 copy-start.3
  5.1 0.0 copy-start.5
  5.1 8.6 %pack.1.send_ref = f32[32,136,128]{2,1,0:T(8,128)S(1)} custom-call(s32[1,2048]{1,0:T(1,128)S(1)} %bitcast.4, s32[1,2048]{1,0:T(1,128)S(1)} %bitcast.5, f32[2,2048]{1,0:T(2,128)S(1)} %copy-done.4, f32[64,2048]{1,0:T(8,128)S(1)} %copy-done.1, f32[64,2048]{1,0:T(8,128)S(1)} %copy-done.2), custom_call_target="tpu_custom_call" | custom-call | tf_op jit(solution)/shard_map/pack/pallas_call | solution.py:341
  13.7 0.0 copy-done
  13.7 0.0 copy-done.3
  13.7 0.0 copy-done.5
  13.8 130.7 %main.1 = f32[64,16,128]{2,1,0:T(8,128)S(1)} custom-call(f32[32,136,128]{2,1,0:T(8,128)S(1)} %pack.1.send_ref, f32[64,16,128]{2,1,0:T(8,128)S(1)} %copy-done, f32[2,16,128]{2,1,0:T(8,128)S(1)} %copy-done.5, f32[64,64]{1,0:T(8,128)S(1)} %copy-done.3, f32[64,64]{1,0:T(8,128)S(1)} %bitcast.3), custom_call_target="tpu_custom_call" | custom-call | tf_op jit(solution)/shard_map/main/pallas_call | solution.py:351
  144.5 0.9 add.3
Async XLA Ops:
  0.0 13.7 %copy-start = (f32[64,16,128]{2,1,0:T(8,128)S(1)}, f32[64,16,128]{2,1,0:T(8,128)}, u32[]{:S(2)}) copy-start(f32[64,16,128]{2,1,0:T(8,128)} %control_ref.1) | copy-start | bytes 1572868
  0.9 1.1 copy-start.1
  1.9 1.0 copy-start.2
  3.0 0.7 copy-start.4
  3.7 0.7 copy-start.6
  4.4 0.7 copy-start.7
  5.1 8.6 %copy-start.3 = (f32[64,64]{1,0:T(8,128)S(1)}, f32[64,64]{1,0:T(8,128)}, u32[]{:S(2)}) copy-start(f32[64,64]{1,0:T(8,128)} %vert_ref.1) | copy-start | bytes 49156
  5.1 8.6 %copy-start.5 = (f32[2,16,128]{2,1,0:T(8,128)S(1)}, f32[2,16,128]{2,1,0:T(8,128)}, u32[]{:S(2)}) copy-start(f32[2,16,128]{2,1,0:T(8,128)} %kappa_ref.1) | copy-start | bytes 49156

commit v2 on v1

--- a/solution.py
+++ b/solution.py
@@ -67,12 +67,13 @@
 def main_kernel(
     n_lat, n_lon, send_ref, control_ref, kappa_ref, vert_ref, vert_t_ref, out_ref,
     recv, ext, side, edges, near, coef, wide, s4, a4, row_out, row_in, col_out, col_in,
-    ext2, side2, edges2, near2,
-    a_send, a_recv, own_sem, lat_send, lat_recv, lon_send, lon_recv, st_send, st_recv,
+    ext2, side2, edges2, near2, hots, w8,
+    a_send, a_recv, own_sem, lat_send, lat_recv, lon_send, lon_recv,
     ad_send, ad_recv, lat2_send, lat2_recv, lon2_send, lon2_recv,
 ):
     devices, _, cap = recv.shape
     lev, rows, cols = control_ref.shape
+    sent = 2 * lev + 3
     lat, lon = lax.axis_index("lat"), lax.axis_index("lon")
     me = lat * n_lon + lon
     top = lat == n_lat - 1
@@ -82,7 +83,10 @@
         return (lax.rem(lat + dy + n_lat, n_lat), lax.rem(lon + dx + n_lon, n_lon))
 
     def at_distance(k):
-        d = lax.rem(me + k, devices)
+        d, bit = 0, 1
+        while bit < devices:
+            d = d + bit * lax.rem(me // bit + k // bit, 2)
+            bit *= 2
         return d // n_lon, lax.rem(d, n_lon), d
 
     barrier = pltpu.get_barrier_semaphore()
@@ -98,25 +102,29 @@
     def obs_copy(k):
         y, x, d = at_distance(k)
         return pltpu.make_async_remote_copy(
-            src_ref=send_ref.at[d], dst_ref=recv.at[k], send_sem=a_send.at[k],
+            src_ref=send_ref.at[d, pl.ds(0, sent)], dst_ref=recv.at[k, pl.ds(0, sent)], send_sem=a_send.at[k],
             recv_sem=a_recv.at[k], device_id=(y, x), device_id_type=MESH,
         )
 
     lane = lax.broadcasted_iota(jnp.int32, (1, cols), 1)
 
-    def edge_block(values):
-        acc = jnp.zeros(values[0].shape, F32)
-        for r, x in enumerate(values):
-            acc = jnp.where((lane >= 4 * r) & (lane < 4 * r + 4), pltpu.roll(x, (4 * r + 4) % cols, 1), acc)
-            b = 64 + 4 * r
-            acc = jnp.where((lane >= b) & (lane < b + 4), pltpu.roll(x, b % cols, 1), acc)
-        return acc
+    def edge_blocks(edges_, ext_):
+        east = jnp.zeros(edges_.shape[1:], F32)
+        west = jnp.zeros(edges_.shape[1:], F32)
+        for r in range(rows):
+            x = ext_[r + 4]
+            a, b = 4 * r, 5 * r
+            east = jnp.where((lane >= a) & (lane < a + 4), pltpu.roll(x, (a + 4) % cols, 1), east)
+            west = jnp.where((lane >= b) & (lane < b + 5), pltpu.roll(x, b % cols, 1), west)
+        edges_[0] = east
+        edges_[1] = west
 
     def halo_copies(ext_, edges_, near_, sems):
         ls, lr, os, orr = sems
+        more = ext_.shape[0] - rows - 4
         copies = [
             pltpu.make_async_remote_copy(
-                src_ref=ext_.at[pl.ds(4, 4)], dst_ref=ext_.at[pl.ds(rows + 4, 4)], send_sem=ls.at[0],
+                src_ref=ext_.at[pl.ds(4, more)], dst_ref=ext_.at[pl.ds(rows + 4, more)], send_sem=ls.at[0],
                 recv_sem=lr.at[0], device_id=to(-1, 0), device_id_type=MESH),
             pltpu.make_async_remote_copy(
                 src_ref=ext_.at[pl.ds(rows, 4)], dst_ref=ext_.at[pl.ds(0, 4)], send_sem=ls.at[1],
@@ -124,19 +132,19 @@
         ]
         for j, (dy, dx) in enumerate(SIDES):
             copies.append(pltpu.make_async_remote_copy(
-                src_ref=edges_, dst_ref=near_.at[j], send_sem=os.at[j], recv_sem=orr.at[j],
+                src_ref=edges_.at[0 if dx < 0 else 1], dst_ref=near_.at[j], send_sem=os.at[j], recv_sem=orr.at[j],
                 device_id=to(-dy, -dx), device_id_type=MESH))
         return copies
 
     def build_side(near_, side_):
-        for r in range(rows + 8):
+        for r in range(side_.shape[0]):
             q = r - 4
             dy = 0 if 0 <= q < rows else (-1 if q < 0 else 1)
             rr = q - dy * rows
             east = near_[SIDES.index((dy, 1))]
             west = near_[SIDES.index((dy, -1))]
             side_[r] = jnp.where(
-                lane < 4, pltpu.roll(east, (cols - 64 - 4 * rr) % cols, 1),
+                lane < 5, pltpu.roll(east, (cols - 5 * rr) % cols, 1),
                 jnp.where(lane >= cols - 4, pltpu.roll(west, (cols - 4 - 4 * rr) % cols, 1), 0.0))
 
     def ring(m, s, step):
@@ -148,21 +156,22 @@
     def smooth(main_, side_, put):
         def body(b, _):
             lv = pl.ds(pl.multiple_of(b * 8, 8), 8)
-            m = [main_[r, lv, :] for r in range(rows + 8)]
-            s = [side_[r, lv, :] for r in range(rows + 8)]
+            total = main_.shape[0]
+            extra = total - rows - 8
+            m = [main_[r, lv, :] for r in range(total)]
+            s = [side_[r, lv, :] for r in range(total)]
             for step in range(STEPS):
                 nm, ns = list(m), list(s)
-                for r in range(step + 1, rows + 7 - step):
+                for r in range(step + 1, total - 1 - step):
                     em, es = ring(m[r], s[r], 1)
                     wm, ws = ring(m[r], s[r], -1)
                     nm[r] = (coef[0, r] * m[r] + coef[1, r] * em + coef[2, r] * wm
                              + coef[3, r] * m[r + 1] + coef[3, r - 1] * m[r - 1])
-                    if step < STEPS - 1:
+                    if step < STEPS - 1 or extra:
                         ns[r] = (coef[4, r] * s[r] + coef[5, r] * es + coef[6, r] * ws
                                  + coef[7, r] * s[r + 1] + coef[7, r - 1] * s[r - 1])
                 m, s = nm, ns
-            for r in range(rows):
-                put(lv, r, m[r + 4])
+            put(lv, m[4 : 4 + rows + extra], s[4 : 4 + rows + extra])
             return 0
 
         lax.fori_loop(0, lev // 8, body, 0)
@@ -174,7 +183,7 @@
         if r == rows - 1:
             north = jnp.where(top, 0.0, north)
         ext[r + 4, lev : lev + 8, :] = jnp.concatenate([kappa_ref[0, r : r + 1, :], north, zero6], 0)
-    edges[...] = edge_block([ext[r + 4] for r in range(rows)])
+    edge_blocks(edges, ext)
     first = halo_copies(ext, edges, near, (lat_send, lat_recv, lon_send, lon_recv))
     for c in first:
         c.start()
@@ -193,7 +202,7 @@
     def spread(x):
         return jnp.broadcast_to(x, (8, cols))
 
-    for r in range(rows + 8):
+    for r in range(rows + 9):
         km, ks = ext[r, lev : lev + 8, :], side[r, lev : lev + 8, :]
         em, es = spread(km[0:1]), spread(ks[0:1])
         wm, ws = ring(em, es, -1)
@@ -204,8 +213,12 @@
             coef[0, r] = 1.0 - em - wm - nm - coef[3, r - 1]
             coef[4, r] = 1.0 - es - ws - ns - coef[7, r - 1]
 
-    def put_wide(lv, r, x):
-        wide[lv, r * cols : (r + 1) * cols] = x
+    def put_wide(lv, main_rows, side_rows):
+        acc = jnp.zeros((8, cols), F32)
+        for r in range(rows + 1):
+            wide[lv, r * cols : (r + 1) * cols] = main_rows[r]
+            acc = jnp.where(lane == r, pltpu.roll(side_rows[r], r, 1), acc)
+        wide[lv, (rows + 1) * cols : (rows + 2) * cols] = acc
 
     smooth(ext, side, put_wide)
     wide[...] = jnp.dot(vert_ref[...], wide[...], precision=lax.Precision.HIGHEST, preferred_element_type=F32)
@@ -213,32 +226,21 @@
     def row(r):
         return wide[:, r * cols : (r + 1) * cols]
 
-    row_out[0] = row(0)
-    acc = jnp.zeros((lev, cols), F32)
-    for r in range(rows):
-        acc = jnp.where(lane == r, pltpu.roll(row(r), r, 1), acc)
-    col_out[0] = acc
-
-    def trio(which, sign, sems, semr):
+    def trio(sign, sems, semr):
         return [
             pltpu.make_async_remote_copy(
-                src_ref=row_out.at[which], dst_ref=row_in.at[which], send_sem=sems.at[0], recv_sem=semr.at[0],
+                src_ref=row_out, dst_ref=row_in, send_sem=sems.at[0], recv_sem=semr.at[0],
                 device_id=to(sign, 0), device_id_type=MESH),
             pltpu.make_async_remote_copy(
-                src_ref=col_out.at[which], dst_ref=col_in.at[which, 0], send_sem=sems.at[1], recv_sem=semr.at[1],
+                src_ref=col_out, dst_ref=col_in.at[0], send_sem=sems.at[1], recv_sem=semr.at[1],
                 device_id=to(0, sign), device_id_type=MESH),
             pltpu.make_async_remote_copy(
-                src_ref=col_out.at[which], dst_ref=col_in.at[which, 1], send_sem=sems.at[2], recv_sem=semr.at[2],
+                src_ref=col_out, dst_ref=col_in.at[1], send_sem=sems.at[2], recv_sem=semr.at[2],
                 device_id=to(sign, sign), device_id_type=MESH),
         ]
 
-    second = trio(0, -1, st_send, st_recv)
-    for c in second:
-        c.start()
-    for c in second:
-        c.wait()
-    last_row = jnp.where(top, 0.0, row_in[0])
-    last_corner = jnp.where(top, 0.0, col_in[0, 1])
+    last_row = jnp.where(top, 0.0, row(rows))
+    east_col = jnp.where(top & (lane == rows), 0.0, row(rows + 1))
 
     def put_s4(corner, r, x):
         hi, lo = split_two(x)
@@ -247,7 +249,7 @@
 
     for r in range(rows + 1):
         x = row(r) if r < rows else last_row
-        over = pltpu.roll(col_in[0, 0], cols - 1 - r, 1) if r < rows else pltpu.roll(last_corner, cols - 1, 1)
+        over = pltpu.roll(east_col, cols - 1 - r, 1)
         e = jnp.where(lane == cols - 1, over, pltpu.roll(x, cols - 1, 1))
         if r < rows:
             put_s4(0, r, x)
@@ -260,7 +262,16 @@
     own.wait()
     group = max(1, 256 // cap)
 
-    def work(g, _):
+    width = group * cap
+    inner = hots.shape[1] // width
+
+    def work(batch, _):
+        lax.fori_loop(0, inner, lambda i, c: one_group(batch * inner + i, i), 0)
+        a4[...] += (lax.dot_general(w8[: 4 * lev], hots[...], NT, preferred_element_type=F32)
+                    + lax.dot_general(w8[4 * lev :], hots[...], NT, preferred_element_type=F32))
+        return 0
+
+    def one_group(g, i):
         for j in range(group):
             k = g * group + j
 
@@ -271,19 +282,21 @@
         got = jnp.concatenate([recv[g * group + j] for j in range(group)], 1)
         fx, fy = got[2 * lev : 2 * lev + 1], got[2 * lev + 1 : 2 * lev + 2]
         cell = got[2 * lev + 2 : 2 * lev + 3].astype(jnp.int32)
-        hot = (lax.broadcasted_iota(jnp.int32, (rows * cols, group * cap), 0) == cell).astype(F32).astype(BF)
+        hot = (lax.broadcasted_iota(jnp.int32, (rows * cols, width), 0) == cell).astype(F32).astype(BF)
         m4 = jnp.dot(s4[...], hot, preferred_element_type=F32)
         shares = ((1.0 - fx) * (1.0 - fy), fx * (1.0 - fy), (1.0 - fx) * fy, fx * fy)
-        model = jnp.zeros((lev, group * cap), F32)
+        model = jnp.zeros((lev, width), F32)
         for c, w in enumerate(shares):
             model = model + w * (m4[c * lev : (c + 1) * lev] + m4[(c + 4) * lev : (c + 5) * lev])
         weighted = got[lev : 2 * lev] * (model - got[:lev])
         hi, lo = split_two(jnp.concatenate([w * weighted for w in shares], 0))
-        a4[...] += (lax.dot_general(hi, hot, NT, preferred_element_type=F32)
-                    + lax.dot_general(lo, hot, NT, preferred_element_type=F32))
-        return 0
-
-    lax.fori_loop(0, devices // group, work, 0)
+        at = pl.ds(pl.multiple_of(i * width, width), width)
+        hots[:, at] = hot
+        w8[: 4 * lev, at] = hi
+        w8[4 * lev :, at] = lo
+        return 0
+
+    lax.fori_loop(0, devices // (group * inner), work, 0)
 
     def part(c, r):
         return a4[c * lev : (c + 1) * lev, r * cols : (r + 1) * cols]
@@ -296,22 +309,22 @@
         packed = packed + jnp.where(lane == r, pltpu.roll(e0, r, 1), 0.0)
         packed = packed + jnp.where(lane == r + 1, pltpu.roll(e1, r + 1, 1), 0.0)
         wide[:, r * cols : (r + 1) * cols] = here[r] + above[r - 1] if r else here[r]
-    row_out[1] = above[rows - 1]
-    col_out[1] = packed
-    third = trio(1, 1, ad_send, ad_recv)
+    row_out[...] = above[rows - 1]
+    col_out[...] = packed
+    third = trio(1, ad_send, ad_recv)
     for c in third:
         c.start()
     for c in third:
         c.wait()
-    wide[:, 0:cols] += (jnp.where(bottom, 0.0, row_in[1])
-                        + jnp.where((lane == 0) & jnp.logical_not(bottom), pltpu.roll(col_in[1, 1], cols - rows, 1), 0.0))
+    wide[:, 0:cols] += (jnp.where(bottom, 0.0, row_in[...])
+                        + jnp.where((lane == 0) & jnp.logical_not(bottom), pltpu.roll(col_in[1], cols - rows, 1), 0.0))
     for r in range(rows):
         wide[:, r * cols : (r + 1) * cols] += jnp.where(
-            lane == 0, pltpu.roll(col_in[1, 0], (cols - r) % cols, 1), 0.0)
-    back = jnp.dot(vert_t_ref[...], wide[...], precision=lax.Precision.HIGHEST, preferred_element_type=F32)
+            lane == 0, pltpu.roll(col_in[0], (cols - r) % cols, 1), 0.0)
+    back = jnp.dot(vert_t_ref[...], wide[:, : rows * cols], precision=lax.Precision.HIGHEST, preferred_element_type=F32)
     for r in range(rows):
         ext2[r + 4] = back[:, r * cols : (r + 1) * cols]
-    edges2[...] = edge_block([ext2[r + 4] for r in range(rows)])
+    edge_blocks(edges2, ext2)
     fourth = halo_copies(ext2, edges2, near2, (lat2_send, lat2_recv, lon2_send, lon2_recv))
     for c in fourth:
         c.start()
@@ -319,8 +332,9 @@
         c.wait()
     build_side(near2, side2)
 
-    def put_out(lv, r, x):
-        out_ref[lv, r, :] = x
+    def put_out(lv, main_rows, _side_rows):
+        for r in range(rows):
+            out_ref[lv, r, :] = main_rows[r]
 
     smooth(ext2, side2, put_out)
 
@@ -355,25 +369,27 @@
         out_specs=vmem,
         scratch_shapes=[
             pltpu.VMEM((devices, ROWS_SENT, cap), F32),
-            pltpu.VMEM((rows + 8, lev + 8, cols), F32),
-            pltpu.VMEM((rows + 8, lev + 8, cols), F32),
-            pltpu.VMEM((lev + 8, cols), F32),
+            pltpu.VMEM((rows + 9, lev + 8, cols), F32),
+            pltpu.VMEM((rows + 9, lev + 8, cols), F32),
+            pltpu.VMEM((2, lev + 8, cols), F32),
             pltpu.VMEM((6, lev + 8, cols), F32),
-            pltpu.VMEM((8, rows + 8, 8, cols), F32),
-            pltpu.VMEM((lev, rows * cols), F32),
+            pltpu.VMEM((8, rows + 9, 8, cols), F32),
+            pltpu.VMEM((lev, (rows + 2) * cols), F32),
             pltpu.VMEM((8 * lev, rows * cols), BF),
             pltpu.VMEM((4 * lev, rows * cols), F32),
+            pltpu.VMEM((lev, cols), F32),
+            pltpu.VMEM((lev, cols), F32),
+            pltpu.VMEM((lev, cols), F32),
             pltpu.VMEM((2, lev, cols), F32),
-            pltpu.VMEM((2, lev, cols), F32),
-            pltpu.VMEM((2, lev, cols), F32),
-            pltpu.VMEM((2, 2, lev, cols), F32),
             pltpu.VMEM((rows + 8, lev, cols), F32),
             pltpu.VMEM((rows + 8, lev, cols), F32),
-            pltpu.VMEM((lev, cols), F32),
+            pltpu.VMEM((2, lev, cols), F32),
             pltpu.VMEM((6, lev, cols), F32),
+            pltpu.VMEM((rows * cols, 1024), BF),
+            pltpu.VMEM((8 * lev, 1024), BF),
             dma((devices,)), dma((devices,)), dma,
             dma((2,)), dma((2,)), dma((6,)), dma((6,)),
-            dma((3,)), dma((3,)), dma((3,)), dma((3,)),
+            dma((3,)), dma((3,)),
             dma((2,)), dma((2,)), dma((6,)), dma((6,)),
         ],
         compiler_params=pltpu.CompilerParams(

time: 146 us -> 107 us (0.73)
  Pallas kernels: 139 us -> 100 us
    pallas_call x1, Pallas kernels: 131 us -> 91.8 us  [per_device(): pl.pallas_call(functools.partial(main_kernel, n_lat, n_lon), out_shape=ja...]
where the time goes in v2:
time: 107 us; the launch traced here: 106 us
  Pallas kernels  100 us (93%)
  local copies, waits for them, and re-layouts  5.09 us (5%)
    pallas_call x1, Pallas kernels, per_device(): pl.pallas_call(functools.partial(main_kernel, n_lat, n_lon), out_shape=ja...  91.8 us
    pallas_call x1, Pallas kernels, per_device(): pl.pallas_call(functools.partial(pack_kernel, devices, cap), out_shape=ja...  8.62 us
    unnamed x17, local copies, waits for them, and re-layouts  5.09 us

profile of v2, /device:TPU:0, one launch (start us, length us, event | category | flops | bytes accessed | tf_op | source)
XLA Modules:
  0.0 106.4 jit_solution(10757076237169630225)
XLA Ops:
  0.0 0.0 copy-start
  0.0 0.9 copy.9
  0.9 0.0 copy-start.1
  0.9 1.0 copy-done.1
  1.9 0.0 copy-start.2
  1.9 1.0 copy-done.2
  3.0 0.0 copy-start.4
  3.0 0.7 copy-done.4
  3.7 0.0 copy-start.6
  3.7 0.7 copy-done.6
  4.4 0.0 copy-start.7
  4.4 0.7 copy-done.7
  5.1 0.0 copy-start.3
  5.1 0.0 copy-start.5
  5.1 8.6 %pack.1.send_ref = f32[32,136,128]{2,1,0:T(8,128)S(1)} custom-call(s32[1,2048]{1,0:T(1,128)S(1)} %bitcast.4, s32[1,2048]{1,0:T(1,128)S(1)} %bitcast.5, f32[2,2048]{1,0:T(2,128)S(1)} %copy-done.4, f32[64,2048]{1,0:T(8,128)S(1)} %copy-done.1, f32[64,2048]{1,0:T(8,128)S(1)} %copy-done.2), custom_call_target="tpu_custom_call" | custom-call | tf_op jit(solution)/shard_map/pack/pallas_call | solution.py:355
  13.7 0.0 copy-done
  13.7 0.0 copy-done.3
  13.7 0.0 copy-done.5
  13.8 91.8 %main.1 = f32[64,16,128]{2,1,0:T(8,128)S(1)} custom-call(f32[32,136,128]{2,1,0:T(8,128)S(1)} %pack.1.send_ref, f32[64,16,128]{2,1,0:T(8,128)S(1)} %copy-done, f32[2,16,128]{2,1,0:T(8,128)S(1)} %copy-done.5, f32[64,64]{1,0:T(8,128)S(1)} %copy-done.3, f32[64,64]{1,0:T(8,128)S(1)} %bitcast.3), custom_call_target="tpu_custom_call" | custom-call | tf_op jit(solution)/shard_map/main/pallas_call | solution.py:365
  105.5 0.9 add.3
Async XLA Ops:
  0.0 13.7 %copy-start = (f32[64,16,128]{2,1,0:T(8,128)S(1)}, f32[64,16,128]{2,1,0:T(8,128)}, u32[]{:S(2)}) copy-start(f32[64,16,128]{2,1,0:T(8,128)} %control_ref.1) | copy-start | bytes 1572868
  0.9 1.1 copy-start.1
  1.9 1.0 copy-start.2
  3.0 0.7 copy-start.4
  3.7 0.7 copy-start.6
  4.4 0.7 copy-start.7
  5.1 8.6 %copy-start.3 = (f32[64,64]{1,0:T(8,128)S(1)}, f32[64,64]{1,0:T(8,128)}, u32[]{:S(2)}) copy-start(f32[64,64]{1,0:T(8,128)} %vert_ref.1) | copy-start | bytes 49156
  5.1 8.6 %copy-start.5 = (f32[2,16,128]{2,1,0:T(8,128)S(1)}, f32[2,16,128]{2,1,0:T(8,128)}, u32[]{:S(2)}) copy-start(f32[2,16,128]{2,1,0:T(8,128)} %kappa_ref.1) | copy-start | bytes 49156

commit v3 on v2

--- a/solution.py
+++ b/solution.py
@@ -19,6 +19,14 @@
 def split_two(x):
     hi = x.astype(BF)
     return hi, (x - hi.astype(F32)).astype(BF)
+
+
+def three_products(a, b):
+    n = a.shape[0]
+    ah, al = split_two(a)
+    bh, bl = split_two(b)
+    both = jnp.dot(jnp.concatenate([ah, al], 0), bh, preferred_element_type=F32)
+    return both[:n] + both[n:] + jnp.dot(ah, bl, preferred_element_type=F32)
 
 
 def pack_kernel(tiles, cap, tile_ref, cell_ref, frac_ref, value_ref, prec_ref, out_ref, pay_ref, slot_ref):
@@ -97,7 +105,6 @@
         return 0
 
     lax.fori_loop(1, devices, greet, 0)
-    pl.semaphore_wait(barrier, devices - 1)
 
     def obs_copy(k):
         y, x, d = at_distance(k)
@@ -184,6 +191,7 @@
             north = jnp.where(top, 0.0, north)
         ext[r + 4, lev : lev + 8, :] = jnp.concatenate([kappa_ref[0, r : r + 1, :], north, zero6], 0)
     edge_blocks(edges, ext)
+    pl.semaphore_wait(barrier, devices - 1)
     first = halo_copies(ext, edges, near, (lat_send, lat_recv, lon_send, lon_recv))
     for c in first:
         c.start()
@@ -221,7 +229,7 @@
         wide[lv, (rows + 1) * cols : (rows + 2) * cols] = acc
 
     smooth(ext, side, put_wide)
-    wide[...] = jnp.dot(vert_ref[...], wide[...], precision=lax.Precision.HIGHEST, preferred_element_type=F32)
+    wide[...] = three_products(vert_ref[...], wide[...])
 
     def row(r):
         return wide[:, r * cols : (r + 1) * cols]
@@ -321,7 +329,7 @@
     for r in range(rows):
         wide[:, r * cols : (r + 1) * cols] += jnp.where(
             lane == 0, pltpu.roll(col_in[0], (cols - r) % cols, 1), 0.0)
-    back = jnp.dot(vert_t_ref[...], wide[:, : rows * cols], precision=lax.Precision.HIGHEST, preferred_element_type=F32)
+    back = three_products(vert_t_ref[...], wide[:, : rows * cols])
     for r in range(rows):
         ext2[r + 4] = back[:, r * cols : (r + 1) * cols]
     edge_blocks(edges2, ext2)
@@ -385,8 +393,8 @@
             pltpu.VMEM((rows + 8, lev, cols), F32),
             pltpu.VMEM((2, lev, cols), F32),
             pltpu.VMEM((6, lev, cols), F32),
-            pltpu.VMEM((rows * cols, 1024), BF),
-            pltpu.VMEM((8 * lev, 1024), BF),
+            pltpu.VMEM((rows * cols, 512), BF),
+            pltpu.VMEM((8 * lev, 512), BF),
             dma((devices,)), dma((devices,)), dma,
             dma((2,)), dma((2,)), dma((6,)), dma((6,)),
             dma((3,)), dma((3,)),

time: 107 us -> 105 us (0.981)
    pallas_call x1, Pallas kernels: 91.8 us -> 90.4 us  [per_device(): pl.pallas_call(functools.partial(main_kernel, n_lat, n_lon), out_shape=ja...]
where the time goes in v3:
time: 105 us
  Pallas kernels  99 us (94%)
  local copies, waits for them, and re-layouts  5.09 us (5%)
    pallas_call x1, Pallas kernels, per_device(): pl.pallas_call(functools.partial(main_kernel, n_lat, n_lon), out_shape=ja...  90.4 us
    pallas_call x1, Pallas kernels, per_device(): pl.pallas_call(functools.partial(pack_kernel, devices, cap), out_shape=ja...  8.62 us
    unnamed x17, local copies, waits for them, and re-layouts  5.09 us

profile of v3, /device:TPU:0, one launch (start us, length us, event | category | flops | bytes accessed | tf_op | source)
XLA Modules:
  0.0 105.0 jit_solution(9165416929122334504)
XLA Ops:
  0.0 0.0 copy-start
  0.0 0.9 copy.9
  0.9 0.0 copy-start.1
  0.9 1.0 copy-done.1
  1.9 0.0 copy-start.2
  1.9 1.0 copy-done.2
  3.0 0.0 copy-start.4
  3.0 0.7 copy-done.4
  3.7 0.0 copy-start.6
  3.7 0.7 copy-done.6
  4.4 0.0 copy-start.7
  4.4 0.7 copy-done.7
  5.1 0.0 copy-start.3
  5.1 0.0 copy-start.5
  5.1 8.6 %pack.1.send_ref = f32[32,136,128]{2,1,0:T(8,128)S(1)} custom-call(s32[1,2048]{1,0:T(1,128)S(1)} %bitcast.4, s32[1,2048]{1,0:T(1,128)S(1)} %bitcast.5, f32[2,2048]{1,0:T(2,128)S(1)} %copy-done.4, f32[64,2048]{1,0:T(8,128)S(1)} %copy-done.1, f32[64,2048]{1,0:T(8,128)S(1)} %copy-done.2), custom_call_target="tpu_custom_call" | custom-call | tf_op jit(solution)/shard_map/pack/pallas_call | solution.py:363
  13.7 0.0 copy-done
  13.7 0.0 copy-done.3
  13.7 0.0 copy-done.5
  13.8 90.4 %main.1 = f32[64,16,128]{2,1,0:T(8,128)S(1)} custom-call(f32[32,136,128]{2,1,0:T(8,128)S(1)} %pack.1.send_ref, f32[64,16,128]{2,1,0:T(8,128)S(1)} %copy-done, f32[2,16,128]{2,1,0:T(8,128)S(1)} %copy-done.5, f32[64,64]{1,0:T(8,128)S(1)} %copy-done.3, f32[64,64]{1,0:T(8,128)S(1)} %bitcast.3), custom_call_target="tpu_custom_call" | custom-call | tf_op jit(solution)/shard_map/main/pallas_call | solution.py:373
  104.1 0.9 add.3
Async XLA Ops:
  0.0 13.7 %copy-start = (f32[64,16,128]{2,1,0:T(8,128)S(1)}, f32[64,16,128]{2,1,0:T(8,128)}, u32[]{:S(2)}) copy-start(f32[64,16,128]{2,1,0:T(8,128)} %control_ref.1) | copy-start | bytes 1572868
  0.9 1.1 %copy-start.1 = (f32[64,2048]{1,0:T(8,128)S(1)}, f32[64,2048]{1,0:T(8,128)}, u32[]{:S(2)}) copy-start(f32[64,2048]{1,0:T(8,128)} %value_ref.1) | copy-start | bytes 1572868
  1.9 1.0 copy-start.2
  3.0 0.7 copy-start.4
  3.7 0.7 copy-start.6
  4.4 0.7 copy-start.7
  5.1 8.6 %copy-start.3 = (f32[64,64]{1,0:T(8,128)S(1)}, f32[64,64]{1,0:T(8,128)}, u32[]{:S(2)}) copy-start(f32[64,64]{1,0:T(8,128)} %vert_ref.1) | copy-start | bytes 49156
  5.1 8.6 %copy-start.5 = (f32[2,16,128]{2,1,0:T(8,128)S(1)}, f32[2,16,128]{2,1,0:T(8,128)}, u32[]{:S(2)}) copy-start(f32[2,16,128]{2,1,0:T(8,128)} %kappa_ref.1) | copy-start | bytes 49156
